TPU v7x, 768 devices: a whole 4x8x12 slice. The times are simulated.
768 devices in a mesh: dp: 96 (over z, y), expert: 8 (over x, core).
Axes of the slice: x: 4, y: 8, z: 12, core: 2. Of those that a mesh axis runs over, the one named last changes fastest.
Arguments:
- tokens: bfloat16 [98304, 1024], P(('dp', 'expert')), may hold values from -6 to 6
- cotangent: bfloat16 [98304, 1024], P(('dp', 'expert')), may hold values from -6 to 6
- expert_ids: int32 [98304, 2], P(('dp', 'expert')), may hold values from 0 to 7, all different within a row; in each aligned block of 128 rows (0 to 127, 128 to 255, ...) at most 64 rows name the same one
- route_weights: bfloat16 [98304, 2], P(('dp', 'expert')), may hold values from 0.099609375 to 1
- expert_weights: bfloat16 [8, 1536, 1024], P('expert'), may hold values from -0.1875 to 0.1875
Outputs:
- latent_out: bfloat16 [98304, 1024], P(('dp', 'expert'))
- token_grad: bfloat16 [98304, 1024], P(('dp', 'expert'))
- route_grad: float32 [98304, 2], P(('dp', 'expert'))
- expert_grads: float32 [8, 1536, 1024], P('expert', 'dp')
Inputs may be any that keep to these rules, and one draw needn't show every extreme that they name: `expert_ids`: each token names 2 different experts. In each aligned block of 128 tokens (the tokens of one device) no expert is named by more than 64 tokens, and in some blocks one expert is named by exactly 64.
All inputs are finite; a program needn't handle non-finite values.
Results may differ from a plain program's by a relative error of at most 0.0065.
Values may be sent and summed in bfloat16 or wider, within the bound.
A program may use at most 32 MiB of HBM per device.

v0:
```python
import math

import jax
import jax.numpy as jnp
from jax import lax
from jax.sharding import PartitionSpec as P

HIDDEN_SIZE = 512
CAPACITY = 64


def body(tokens, cotangent, expert_ids, route_weights, expert_weights):
    count_tok, width = tokens.shape
    top_count = expert_ids.shape[1]
    groups = lax.axis_size("expert")
    slot_count = count_tok * top_count
    contract_last = (((1,), (1,)), ((), ()))
    contract_first = (((0,), (0,)), ((), ()))
    flat_ids = expert_ids.reshape(slot_count)
    one_hot = (flat_ids[:, None] == jnp.arange(groups, dtype=jnp.int32)[None, :]).astype(jnp.int32)
    ranks = jnp.sum((jnp.cumsum(one_hot, axis=0) - 1) * one_hot, axis=1)
    target = flat_ids * CAPACITY + ranks
    source_of = (
        jnp.full((groups * CAPACITY,), slot_count, jnp.int32)
        .at[target]
        .set(jnp.arange(slot_count, dtype=jnp.int32))
    )
    token_of = source_of // top_count
    row_data = jnp.concatenate([tokens, cotangent], axis=1)
    padded_rows = jnp.concatenate([row_data, jnp.zeros((1, 2 * width), row_data.dtype)], axis=0)
    send_rows = padded_rows[token_of].reshape(groups, CAPACITY, 2 * width)
    padded_weights = jnp.concatenate(
        [route_weights.reshape(slot_count), jnp.zeros((1,), route_weights.dtype)]
    )
    send_weights = padded_weights[source_of].reshape(groups, CAPACITY)
    recv_rows, recv_weights = (
        lax.all_to_all(send_rows, "expert", split_axis=0, concat_axis=0, tiled=True),
        lax.all_to_all(send_weights, "expert", split_axis=0, concat_axis=0, tiled=True),
    )
    flat_recv = recv_rows.reshape(groups * CAPACITY, 2 * width)
    x_rows = flat_recv[:, :width]
    cot_rows = flat_recv[:, width:]
    weight_rows = recv_weights.reshape(groups * CAPACITY)
    weights = expert_weights[0]
    both = lax.dot_general(
        x_rows, weights[: 2 * HIDDEN_SIZE], contract_last, preferred_element_type=jnp.float32
    )
    pre_gate = both[:, :HIDDEN_SIZE]
    pre_up = both[:, HIDDEN_SIZE:]
    sigmoid_gate = jax.nn.sigmoid(pre_gate)
    gate_act = pre_gate * sigmoid_gate
    hidden = (gate_act * pre_up).astype(jnp.bfloat16)
    slot_out = jnp.dot(
        hidden, weights[2 * HIDDEN_SIZE :], preferred_element_type=jnp.float32
    ).astype(jnp.bfloat16)
    scaled = (weight_rows.astype(jnp.float32)[:, None] * cot_rows.astype(jnp.float32)).astype(
        jnp.bfloat16
    )
    hidden_grad = lax.dot_general(
        scaled, weights[2 * HIDDEN_SIZE :], contract_last, preferred_element_type=jnp.float32
    )
    up_grad = (hidden_grad * gate_act).astype(jnp.bfloat16)
    gate_grad = (
        hidden_grad * pre_up * sigmoid_gate * (1.0 + pre_gate * (1.0 - sigmoid_gate))
    ).astype(jnp.bfloat16)
    both_grad = jnp.concatenate([gate_grad, up_grad], axis=1)
    slot_grad = jnp.dot(
        both_grad, weights[: 2 * HIDDEN_SIZE], preferred_element_type=jnp.float32
    ).astype(jnp.bfloat16)
    back_rows = jnp.concatenate([slot_out, slot_grad], axis=1).reshape(groups, CAPACITY, 2 * width)
    returned = lax.all_to_all(back_rows, "expert", split_axis=0, concat_axis=0, tiled=True)
    per_slot = returned.reshape(groups * CAPACITY, 2 * width)[target].reshape(
        count_tok, top_count, 2 * width
    )
    out_slots = per_slot[:, :, :width].astype(jnp.float32)
    grad_slots = per_slot[:, :, width:].astype(jnp.float32)
    latent_out = jnp.sum(route_weights.astype(jnp.float32)[:, :, None] * out_slots, axis=1).astype(
        jnp.bfloat16
    )
    token_grad = jnp.sum(grad_slots, axis=1).astype(jnp.bfloat16)
    route_grad = jnp.sum(cotangent.astype(jnp.float32)[:, None, :] * out_slots, axis=2)
    total_tokens = count_tok * lax.axis_size("dp") * groups
    factor = 1.0 / math.sqrt(total_tokens)
    term = jnp.concatenate(
        [
            lax.dot_general(both_grad, x_rows, contract_first, preferred_element_type=jnp.float32),
            lax.dot_general(hidden, scaled, contract_first, preferred_element_type=jnp.float32),
        ],
        axis=0,
    )
    summed = lax.psum_scatter(term, "dp", scatter_dimension=0, tiled=True)
    expert_grads = (summed * factor)[None]
    return (latent_out, token_grad, route_grad, expert_grads)


def solution(mesh):
    return jax.shard_map(
        body,
        mesh=mesh,
        in_specs=(
            P(("dp", "expert"), None),
            P(("dp", "expert"), None),
            P(("dp", "expert"), None),
            P(("dp", "expert"), None),
            P("expert", None, None),
        ),
        out_specs=(
            P(("dp", "expert"), None),
            P(("dp", "expert"), None),
            P(("dp", "expert"), None),
            P("expert", "dp", None),
        ),
        check_vma=False,
    )
```

profile of v0, /device:TPU:1, one launch (start us, length us, event | category | flops | bytes accessed | tf_op | source)
XLA Modules:
  0.0 755.8 jit_solution(11629432294659009013)
XLA Ops:
  7.2 0.7 broadcast_multiply_fusion
  7.8 0.8 copy.21
  8.6 0.1 eq.29
  8.8 0.1 eq.25
  8.9 0.8 copy.23
  9.7 0.1 reshape.94
  9.9 0.1 copy.20
  10.0 0.1 mul.73
  10.1 0.6 reduce-window.6
  10.7 0.2 slice_reduce_fusion.1
  11.0 0.1 fusion.24
  11.1 1.4 scatter_custom_fusion
  12.5 3.5 gather_fusion.1
  16.1 0.7 all_to_all.16
  16.7 13.7 %all-to-all-start.1 = ((bf16[8,1,64]{2,1,0:T(2,128)(2,1)}), bf16[8,1,64]{2,1,0:T(2,128)(2,1)S(1)}, u32[]{:S(2)}, u32[]{:S(2)}) async-start(bf16[8,1,64]{2,1,0:T(2,128)(2,1)} %all_to_all.16), calls=%async_computation.1 | async-start | bytes 8192 | tf_op jit(solution)/shard_map/all_to_all | solution.py:38
  30.5 1.1 fusion.22
  31.5 3.3 gather_fusion
  34.9 0.1 all-to-all-done.1
  35.0 4.7 all-to-all-start
  39.7 0.0 reduce-scatter.2.cloned.1.call-start
  39.7 0.1 reshape.98
  39.8 26.2 %all-to-all-done = bf16[8,64,2048]{2,1,0:T(8,128)(2,1)S(1)} async-done(((bf16[8,64,2048]{2,1,0:T(8,128)(2,1)}), bf16[8,64,2048]{2,1,0:T(8,128)(2,1)S(1)}, u32[]{:S(2)}, u32[]{:S(2)}) %all-to-all-start) | async-done | bytes 2097184 | tf_op jit(solution)/shard_map/all_to_all | solution.py:37
  66.0 2.9 fusion.2
  68.9 2.4 multiply_convert_fusion.2
  71.3 0.0 copy-start.3
  71.3 0.8 fusion.23
  72.2 1.3 fusion.17
  73.5 0.0 copy-done.3
  73.5 3.2 pad_maximum_fusion
  76.7 0.0 reduce-scatter.2.cloned.1.call-update
  76.7 0.0 copy-start.4
  76.7 2.0 convolution_convert_fusion
  78.8 0.0 copy-done.4
  78.8 2.9 fusion.6
  81.6 1.5 pad_maximum_fusion.1
  83.2 4.5 all-to-all-start.2
  87.7 0.1 copy.19
  87.8 0.9 convert_element_type.63
  88.7 25.3 %all-to-all-done.2 = bf16[8,64,2048]{2,1,0:T(8,128)(2,1)S(1)} async-done(((bf16[8,64,2048]{2,1,0:T(8,128)(2,1)}), bf16[8,64,2048]{2,1,0:T(8,128)(2,1)S(1)}, u32[]{:S(2)}, u32[]{:S(2)}) %all-to-all-start.2) | async-done | bytes 2097184 | tf_op jit(solution)/shard_map/all_to_all | solution.py:71
  114.0 1.4 gather_fusion.2
  115.4 0.0 copy-start
  115.4 0.7 reshape.97
  116.1 0.3 copy-done
  116.4 2.6 fusion.12
  119.1 0.6 copy.27
  119.7 2.1 slice_reduce_fusion
  121.8 625.6 %reduce-scatter.2.cloned.1.call-done = f32[16,1024]{1,0:T(8,128)} async-done(((f32[1536,1024]{1,0:T(8,128)}), f32[16,1024]{1,0:T(8,128)}) %reduce-scatter.2.cloned.1.call-update) | async-done | bytes 65552 | tf_op jit(solution)/shard_map/reduce_scatter | solution.py:91
  747.5 1.5 multiply_bitcast_fusion
  (14 shorter events, 0.1 us)
Async XLA Ops:
  16.7 18.2 %all-to-all-start.1 = ((bf16[8,1,64]{2,1,0:T(2,128)(2,1)}), bf16[8,1,64]{2,1,0:T(2,128)(2,1)S(1)}, u32[]{:S(2)}, u32[]{:S(2)}) async-start(bf16[8,1,64]{2,1,0:T(2,128)(2,1)} %all_to_all.16), calls=%async_computation.1 | async-start | bytes 8192 | tf_op jit(solution)/shard_map/all_to_all | solution.py:38
  35.0 31.1 %all-to-all-start = ((bf16[8,64,2048]{2,1,0:T(8,128)(2,1)}), bf16[8,64,2048]{2,1,0:T(8,128)(2,1)S(1)}, u32[]{:S(2)}, u32[]{:S(2)}) async-start(bf16[8,64,2048]{2,1,0:T(8,128)(2,1)} %bitcast.4), calls=%async_computation | async-start | bytes 4194304 | tf_op jit(solution)/shard_map/all_to_all | solution.py:37
  39.7 707.7 %reduce-scatter.2.cloned.1.call-start = ((), (), s32[]{:S(2)}) async-start(), calls=%async_computation.4 | async-start | bytes 6356992 | tf_op jit(solution)/shard_map/reduce_scatter | solution.py:91
  71.3 2.2 copy-start.3
  76.7 2.0 copy-start.4
  83.2 4.5 copy-start.2
  83.2 4.6 copy-start.1
  83.2 30.9 %all-to-all-start.2 = ((bf16[8,64,2048]{2,1,0:T(8,128)(2,1)}), bf16[8,64,2048]{2,1,0:T(8,128)(2,1)S(1)}, u32[]{:S(2)}, u32[]{:S(2)}) async-start(bf16[8,64,2048]{2,1,0:T(8,128)(2,1)} %bitcast.32), calls=%async_computation.2 | async-start | bytes 4194304 | tf_op jit(solution)/shard_map/all_to_all | solution.py:71
  115.4 1.0 copy-start
Sparse Core Ops, SparseCore 0:
  76.8 670.5 reduce-scatter.1
where the time goes:
time: 757 us; the launch traced here: 756 us
  waiting for transfers between devices  677 us (89%)
  starting transfers between devices  23 us (3%)
  local copies, waits for them, and re-layouts  14.6 us (2%)
  other arithmetic  14.4 us (2%)
  between operations  14.2 us (2%)
  matrix products  12.3 us (2%)
    reduce_scatter x1, waiting for transfers between devices, body(): summed = lax.psum_scatter(term, 'dp', scatter_dimension=0, tiled=True)  626 us
    all_to_all x1, waiting for transfers between devices, body(): lax.all_to_all(send_rows, 'expert', split_axis=0, concat_axis=0, tiled=True)  26.2 us
    all_to_all x1, waiting for transfers between devices, body(): lax.all_to_all(back_rows, 'expert', split_axis=0, concat_axis=0, tiled=True)  25.3 us
  transfers between devices with their start and end apart: 4, of which 4 were waited for; matrix products, arithmetic and copies ran while one was open for 3% of the time, Pallas kernels for 0%

commit v1 on v0

v1 whole, which is shorter than its diff:
```python
import math

import jax
import jax.numpy as jnp
from jax import lax
from jax.experimental import pallas as pl
from jax.experimental.pallas import tpu as pltpu
from jax.sharding import PartitionSpec as P

MESH = pl.DeviceIdType.MESH
F32 = jnp.float32
BF16 = jnp.bfloat16

HID = 512
CAP = 64
NX = 4
NY = 8
COLS_A = 512
SUBS = 2

NT = (((1,), (1,)), ((), ()))
TN = (((0,), (0,)), ((), ()))


def dot(a, b, dims=(((1,), (0,)), ((), ()))):
    return lax.dot_general(a, b, dims, preferred_element_type=F32)


class Messages:
    def __init__(self, send_sems, recv_sems):
        self.send_sems, self.recv_sems, self.all = send_sems, recv_sems, []

    def start(self, src, dst, device):
        i = len(self.all)
        copy = pltpu.make_async_remote_copy(
            src_ref=src,
            dst_ref=dst,
            send_sem=self.send_sems.at[i],
            recv_sem=self.recv_sems.at[i],
            device_id=device,
            device_id_type=MESH,
        )
        copy.start()
        self.all.append(copy)
        return copy


class Chain:
    def __init__(self, net, pos, n, left, right, term, bufs):
        self.net, self.pos, self.n, self.left, self.right, self.term = net, pos, n, left, right, term
        self.send_r, self.recv_r, self.send_l, self.recv_l = bufs
        self.hr, self.hl = n // 2, n - 1 - n // 2
        self.mr, self.ml = [], []

    def step(self, s):
        if s < self.hr:
            v = self.term(lax.rem(self.pos + self.hr - s, self.n))
            if s:
                self.mr[s - 1].wait_recv()
                v = v + self.recv_r[s - 1].astype(F32)
            self.send_r[s] = v.astype(BF16)
            self.mr.append(self.net.start(self.send_r.at[s], self.recv_r.at[s], self.right))
        if s < self.hl:
            v = self.term(lax.rem(self.pos + self.n - self.hl + s, self.n))
            if s:
                self.ml[s - 1].wait_recv()
                v = v + self.recv_l[s - 1].astype(F32)
            self.send_l[s] = v.astype(BF16)
            self.ml.append(self.net.start(self.send_l.at[s], self.recv_l.at[s], self.left))

    def final(self):
        v = self.term(self.pos)
        self.mr[self.hr - 1].wait_recv()
        v = v + self.recv_r[self.hr - 1].astype(F32)
        if self.hl:
            self.ml[self.hl - 1].wait_recv()
            v = v + self.recv_l[self.hl - 1].astype(F32)
        return v


def kernel(
    nz, factor,
    tok, cot, ids, wts, ew,
    lat_o, tg_o, rg_o, eg_o,
    weights, tok_b, cot_b, route_b, pick_b, rhs_b, cot_s, grad_s,
    con_l, con_g, sib_l, sib_g, part_l, part_g, xin, rg_s, rg_r,
    term_b, asr, arr, asl, arl, bsr, brr, bsl, brl, sum_a, sum_b, two_a, two_b, in_a, in_b,
    local_sem, send_sems, recv_sems,
):
    dp, ex = lax.axis_index("dp"), lax.axis_index("expert")
    z, y = lax.div(dp, NY), lax.rem(dp, NY)
    x, c = lax.div(ex, 2), lax.rem(ex, 2)

    def in_group(dx, dc):
        return {"dp": dp, "expert": lax.rem(x + dx + NX, NX) * 2 + lax.rem(c + dc, 2)}

    def along_y(d):
        return {"dp": z * NY + lax.rem(y + d + NY, NY), "expert": ex}

    def along_z(d):
        return {"dp": lax.rem(z + d + nz, nz) * NY + y, "expert": ex}

    offset = (0, -1, 1, 2)
    inverse = (0, 2, 1, 3)

    load = pltpu.make_async_copy(ew, weights, local_sem)
    load.start()
    expert_of = lax.broadcasted_iota(jnp.int32, (8, 128), 0)
    w_in = wts[...].astype(F32)
    id_in = ids[...]
    route_b[0] = sum(
        jnp.where(id_in[k : k + 1] == expert_of, w_in[k : k + 1], 0.0) for k in range(2)
    )

    barrier = pltpu.get_barrier_semaphore()
    partners = (
        [in_group(offset[k % 4], k // 4) for k in range(1, 8)]
        + [along_y(d) for d in range(1, NY)]
        + [along_z(d) for d in range(1, nz)]
    )
    for device in partners:
        pl.semaphore_signal(barrier, inc=1, device_id=device, device_id_type=MESH)
    pl.semaphore_wait(barrier, len(partners))

    net = Messages(send_sems, recv_sems)
    right, left, sibling = in_group(1, 0), in_group(-1, 0), in_group(0, 1)

    route_in = [
        net.start(route_b.at[0], route_b.at[inverse[k % 4] + k // 4 * 4], in_group(offset[k % 4], k // 4))
        for k in range(1, 8)
    ]
    sib_t, sib_c = [None] * 4, [None] * 4
    tok_l = net.start(tok, tok_b.at[0], right)
    cot_r = net.start(cot, cot_b.at[1], left)
    sib_t[0] = net.start(tok, tok_b.at[3], sibling)
    sib_c[0] = net.start(cot, cot_b.at[3], sibling)
    cot_l = net.start(cot, cot_b.at[0], right)
    tok_r = net.start(tok, tok_b.at[1], left)

    def block(k):
        return (tok, cot) if k == 0 else (tok_b.at[k - 1], cot_b.at[k - 1])

    for m in route_in:
        m.wait_recv()
    rows = jnp.concatenate([route_b[k, pl.ds(ex, 1), :] for k in range(8)], axis=0)
    before = (
        lax.broadcasted_iota(jnp.int32, (128, 128), 0) < lax.broadcasted_iota(jnp.int32, (128, 128), 1)
    ).astype(F32)
    ranks = dot(jnp.where(rows > 0, 1.0, 0.0).astype(BF16), before.astype(BF16))
    seat = lax.broadcasted_iota(jnp.int32, (CAP, 128), 0).astype(F32)
    load.wait()

    def stage(slots, base):
        size = CAP * len(slots)
        own = pl.ds(base, size)
        w_of = []
        for i, k in enumerate(slots):
            at = pl.ds(base + CAP * i, CAP)
            pick = jnp.where((ranks[k : k + 1] == seat) & (rows[k : k + 1] > 0), 1.0, 0.0)
            w = jnp.sum(pick * rows[k : k + 1], axis=1, keepdims=True)
            w_of.append(w)
            pick = pick.astype(BF16)
            pick_b[k] = pick
            t_ref, c_ref = block(k)
            rhs_b[0, at, :] = dot(pick, t_ref[...]).astype(BF16)
            cots = dot(pick, c_ref[...])
            cot_s[at, :] = cots.astype(BF16)
            rhs_b[1, at, :] = (w * cots).astype(BF16)
        w = jnp.concatenate(w_of, axis=0)
        both = dot(rhs_b[0, own, :], weights[: 2 * HID, :], NT)
        gate, up = both[:, :HID], both[:, HID:]
        sig = 1.0 / (1.0 + jnp.exp(-gate))
        act = gate * sig
        hidden = (act * up).astype(BF16)
        grad_s[own, 2 * HID :] = hidden
        d_hidden = dot(rhs_b[1, own, :], weights[2 * HID :, :], NT)
        grad_s[own, HID : 2 * HID] = (d_hidden * act).astype(BF16)
        grad_s[own, :HID] = (d_hidden * up * sig * (1.0 + gate * (1.0 - sig))).astype(BF16)
        out = dot(hidden, weights[2 * HID :, :]).astype(BF16).astype(F32)
        r_grad = jnp.sum(cot_s[own, :].astype(F32) * out, axis=1, keepdims=True)
        out = (w * out).astype(BF16)
        d_x = dot(grad_s[own, : 2 * HID], weights[: 2 * HID, :]).astype(BF16)
        for i, k in enumerate(slots):
            pick = pick_b[k]
            part = slice(CAP * i, CAP * (i + 1))
            con_l[k] = dot(pick, out[part], TN).astype(BF16)
            con_g[k] = dot(pick, d_x[part], TN).astype(BF16)
            line = jnp.sum(pick.astype(F32) * r_grad[part], axis=0, keepdims=True)
            rg_s[k] = jnp.broadcast_to(line, (8, 128))

    sib_out = {}

    def to_sibling(k):
        sib_out[k] = (
            net.start(con_l.at[k + 4], sib_l.at[k], sibling),
            net.start(con_g.at[k + 4], sib_g.at[k], sibling),
        )

    def chip_part(k):
        for m in sib_out[k]:
            m.wait_recv()
        part_l[k] = (con_l[k].astype(F32) + sib_l[k].astype(F32)).astype(BF16)
        part_g[k] = (con_g[k].astype(F32) + sib_g[k].astype(F32)).astype(BF16)

    sib_t[0].wait_recv()
    sib_c[0].wait_recv()
    stage((0, 4), 0)
    to_sibling(0)

    tok_l.wait_recv()
    opp_t = net.start(tok_b.at[0], tok_b.at[2], right)
    sib_t[1] = net.start(tok_b.at[0], tok_b.at[4], sibling)
    cot_r.wait_recv()
    opp_c = net.start(cot_b.at[1], cot_b.at[2], left)
    sib_c[2] = net.start(cot_b.at[1], cot_b.at[5], sibling)
    cot_l.wait_recv()
    sib_c[1] = net.start(cot_b.at[0], cot_b.at[4], sibling)
    tok_r.wait_recv()
    sib_t[2] = net.start(tok_b.at[1], tok_b.at[5], sibling)
    for k in (1, 2):
        sib_t[k].wait_recv()
        sib_c[k].wait_recv()
    stage((1, 2, 5, 6), 2 * CAP)
    to_sibling(1)
    to_sibling(2)
    opp_t.wait_recv()
    sib_t[3] = net.start(tok_b.at[2], tok_b.at[6], sibling)
    opp_c.wait_recv()
    sib_c[3] = net.start(cot_b.at[2], cot_b.at[6], sibling)
    chip_part(1)
    chip_part(2)
    near_g = net.start(part_g.at[2], xin.at[0], right)
    near_l = net.start(part_l.at[1], xin.at[1], left)
    sib_t[3].wait_recv()
    sib_c[3].wait_recv()
    stage((3, 7), 6 * CAP)
    to_sibling(3)

    def term_of(i, carry):
        at = pl.multiple_of(i * 128, 128)
        t = dot(grad_s[:, pl.ds(at, 128)], rhs_b[lax.div(at, 2 * HID)], TN)
        term_b[i] = t.reshape(NY, 16, t.shape[1])
        return carry

    lax.fori_loop(0, nz, term_of, 0)

    wide_a, wide_b = asr.shape[-1], bsr.shape[-1]

    def chain_a(q):
        def term(t):
            return term_b[:, t, :, q * wide_a : (q + 1) * wide_a]

        bufs = [b.at[q] for b in (asr, arr, asl, arl)]
        return Chain(net, y, NY, along_y(-1), along_y(1), term, bufs)

    def chain_b(q):
        def term(t):
            return term_b[t, :, :, COLS_A + q * wide_b : COLS_A + (q + 1) * wide_b]

        bufs = [b.at[q] for b in (bsr, brr, bsl, brl)]
        return Chain(net, z, nz, along_z(-1), along_z(1), term, bufs)

    chains_a = [chain_a(q) for q in range(SUBS)]
    chains_b = [chain_b(q) for q in range(SUBS)]

    def ring(s):
        for q in range(SUBS):
            chains_a[q].step(s)
            chains_b[q].step(s)

    ring(0)
    chip_part(3)
    far_l = net.start(part_l.at[3], xin.at[2], right)
    far_g = net.start(part_g.at[3], xin.at[3], left)
    rg_in = [
        net.start(rg_s.at[k], rg_r.at[inverse[k % 4] + k // 4 * 4], in_group(offset[k % 4], k // 4))
        for k in range(1, 8)
    ]
    ring(1)
    ring(2)
    far_l.wait_recv()
    part_l[2] = (part_l[2].astype(F32) + xin[2].astype(F32)).astype(BF16)
    last_l = net.start(part_l.at[2], xin.at[4], right)
    far_g.wait_recv()
    part_g[1] = (part_g[1].astype(F32) + xin[3].astype(F32)).astype(BF16)
    last_g = net.start(part_g.at[1], xin.at[5], left)
    ring(3)
    chip_part(0)
    for q in range(SUBS):
        sum_a[:, :, q * wide_a : (q + 1) * wide_a] = chains_a[q].final()
    two_a[...] = sum_a[...].astype(BF16)
    a_in = [
        net.start(two_a.at[lax.rem(z + d, nz)], in_a.at[d - 1], along_z(d)) for d in range(1, nz)
    ]
    for s in range(4, nz // 2):
        ring(s)
    for q in range(SUBS):
        sum_b[:, :, q * wide_b : (q + 1) * wide_b] = chains_b[q].final()
    two_b[...] = sum_b[...].astype(BF16)
    b_in = [
        net.start(two_b.at[lax.rem(y + d, NY)], in_b.at[d - 1], along_y(d)) for d in range(1, NY)
    ]

    near_g.wait_recv()
    last_g.wait_recv()
    tg_o[...] = (part_g[0].astype(F32) + xin[0].astype(F32) + xin[5].astype(F32)).astype(BF16)
    near_l.wait_recv()
    last_l.wait_recv()
    lat_o[...] = (part_l[0].astype(F32) + xin[1].astype(F32) + xin[4].astype(F32)).astype(BF16)
    route = [jnp.zeros((1, 128), F32), jnp.zeros((1, 128), F32)]
    for m in rg_in:
        m.wait_recv()
    for k in range(8):
        line = rg_s[0, 0:1, :] if k == 0 else rg_r[k, 0:1, :]
        expert = in_group(offset[k % 4], k // 4)["expert"]
        for j in range(2):
            route[j] = route[j] + jnp.where(id_in[j : j + 1] == expert, line, 0.0)
    rg_o[...] = jnp.concatenate(route, axis=0)

    for m in a_in:
        m.wait_recv()
    eg_o[:, :COLS_A] = factor * (sum_a[z] + jnp.sum(in_a[...].astype(F32), axis=0))
    for m in b_in:
        m.wait_recv()
    eg_o[:, COLS_A:] = factor * (sum_b[y] + jnp.sum(in_b[...].astype(F32), axis=0))
    for m in net.all:
        m.wait_send()


def solution(mesh):
    n_dp, n_ex = mesh.shape["dp"], mesh.shape["expert"]
    nz = n_dp // NY

    def body(tokens, cotangent, expert_ids, route_weights, expert_weights):
        count, width = tokens.shape
        slots = CAP * n_ex
        factor = 1.0 / math.sqrt(count * n_dp * n_ex)
        wide_a, wide_b = COLS_A // SUBS, (width - COLS_A) // SUBS
        hr_a, hl_a = NY // 2, NY - 1 - NY // 2
        hr_b, hl_b = nz // 2, nz - 1 - nz // 2
        vmem = pl.BlockSpec(memory_space=pltpu.VMEM)
        count_messages = 7 + 6 + 6 + 2 + 8 + 6 + 7 + SUBS * (NY - 1 + nz - 1) + nz - 1 + NY - 1
        lat, tg, rg, eg = pl.pallas_call(
            lambda *refs: kernel(nz, factor, *refs),
            out_shape=(
                jax.ShapeDtypeStruct((count, width), BF16),
                jax.ShapeDtypeStruct((count, width), BF16),
                jax.ShapeDtypeStruct((2, count), F32),
                jax.ShapeDtypeStruct((16, width), F32),
            ),
            in_specs=[vmem, vmem, vmem, vmem, pl.BlockSpec(memory_space=pl.ANY)],
            out_specs=(vmem,) * 4,
            scratch_shapes=[
                pltpu.VMEM((3 * HID, width), BF16),
                pltpu.VMEM((7, count, width), BF16),
                pltpu.VMEM((7, count, width), BF16),
                pltpu.VMEM((8, 8, 128), F32),
                pltpu.VMEM((8, CAP, 128), BF16),
                pltpu.VMEM((2, slots, width), BF16),
                pltpu.VMEM((slots, width), BF16),
                pltpu.VMEM((slots, 3 * HID), BF16),
                pltpu.VMEM((8, count, width), BF16),
                pltpu.VMEM((8, count, width), BF16),
                pltpu.VMEM((4, count, width), BF16),
                pltpu.VMEM((4, count, width), BF16),
                pltpu.VMEM((4, count, width), BF16),
                pltpu.VMEM((4, count, width), BF16),
                pltpu.VMEM((6, count, width), BF16),
                pltpu.VMEM((8, 8, 128), F32),
                pltpu.VMEM((8, 8, 128), F32),
                pltpu.VMEM((nz, NY, 16, width), F32),
                pltpu.VMEM((SUBS, hr_a, nz, 16, wide_a), BF16),
                pltpu.VMEM((SUBS, hr_a, nz, 16, wide_a), BF16),
                pltpu.VMEM((SUBS, hl_a, nz, 16, wide_a), BF16),
                pltpu.VMEM((SUBS, hl_a, nz, 16, wide_a), BF16),
                pltpu.VMEM((SUBS, hr_b, NY, 16, wide_b), BF16),
                pltpu.VMEM((SUBS, hr_b, NY, 16, wide_b), BF16),
                pltpu.VMEM((SUBS, hl_b, NY, 16, wide_b), BF16),
                pltpu.VMEM((SUBS, hl_b, NY, 16, wide_b), BF16),
                pltpu.VMEM((nz, 16, COLS_A), F32),
                pltpu.VMEM((NY, 16, width - COLS_A), F32),
                pltpu.VMEM((nz, 16, COLS_A), BF16),
                pltpu.VMEM((NY, 16, width - COLS_A), BF16),
                pltpu.VMEM((nz - 1, 16, COLS_A), BF16),
                pltpu.VMEM((NY - 1, 16, width - COLS_A), BF16),
                pltpu.SemaphoreType.DMA,
                pltpu.SemaphoreType.DMA((count_messages,)),
                pltpu.SemaphoreType.DMA((count_messages,)),
            ],
            compiler_params=pltpu.CompilerParams(
                collective_id=0, has_side_effects=True, vmem_limit_bytes=60 * 1024 * 1024
            ),
        )(
            tokens,
            cotangent,
            expert_ids.T,
            route_weights.T,
            expert_weights.reshape(expert_weights.shape[1:]),
        )
        return lat, tg, rg.T, eg[None]

    return jax.shard_map(
        body,
        mesh=mesh,
        in_specs=(
            P(("dp", "expert"), None),
            P(("dp", "expert"), None),
            P(("dp", "expert"), None),
            P(("dp", "expert"), None),
            P("expert", None, None),
        ),
        out_specs=(
            P(("dp", "expert"), None),
            P(("dp", "expert"), None),
            P(("dp", "expert"), None),
            P("expert", "dp", None),
        ),
        check_vma=False,
    )
```

time: 757 us -> 94.5 us (0.12)
  the two profiles are of different devices: /device:TPU:1 before, /device:TPU:8 now
where the time goes in v1:
time: 94.5 us; the launch traced here: 94.2 us
  Pallas kernels  87.6 us (93%)
  local copies, waits for them, and re-layouts  6.04 us (6%)
    pallas_call x1, Pallas kernels, body(): pl.pallas_call(lambda *refs: kernel(nz, factor, *refs), out_shape=(jax.Sh...  87.6 us
    unnamed x4, local copies, waits for them, and re-layouts  6.04 us

profile of v1, /device:TPU:8, one launch (start us, length us, event | category | flops | bytes accessed | tf_op | source)
XLA Modules:
  0.0 94.2 jit_solution(17415962913090327709)
XLA Ops:
  0.6 87.6 %shard_map.84 = (bf16[128,1024]{1,0:T(8,128)(2,1)}, bf16[128,1024]{1,0:T(8,128)(2,1)}, f32[2,128]{1,0:T(2,128)}, f32[16,1024]{1,0:T(8,128)}) custom-call(bf16[128,1024]{1,0:T(8,128)(2,1)} %refs_0_.1, bf16[128,1024]{1,0:T(8,128)(2,1)} %refs_1_.1, s32[2,128]{1,0:T(2,128)} %bitcast.7, bf16[2,128]{1,0:T(2,128)(2,1)} %bitcast.9, bf16[1536,1024]{1,0:T(8,128)(2,1)} %bitcast.5), custom_call_target="tpu_custom_call" | custom-call | tf_op jit(solution)/shard_map/pallas_call | solution.py:343
  88.2 1.7 %copy.13 = bf16[128,1024]{1,0:T(8,128)(2,1)} copy(bf16[128,1024]{1,0:T(8,128)(2,1)} %get-tuple-element.16) | data formatting | bytes 524288
  89.9 1.7 %copy.14 = bf16[128,1024]{1,0:T(8,128)(2,1)} copy(bf16[128,1024]{1,0:T(8,128)(2,1)} %get-tuple-element.17) | data formatting | bytes 524288
  91.5 1.2 %copy.15 = f32[128,2]{0,1:T(2,128)} copy(f32[128,2]{0,1:T(2,128)} %bitcast.8) | data formatting | bytes 2048
  92.8 1.5 %copy.16 = f32[1,16,1024]{2,1,0:T(8,128)} copy(f32[1,16,1024]{2,1,0:T(8,128)} %bitcast.6) | data formatting | bytes 131072

commit v2 on v1

--- a/solution.py
+++ b/solution.py
@@ -15,8 +15,11 @@
 CAP = 64
 NX = 4
 NY = 8
-COLS_A = 512
-SUBS = 2
+WIDE = 128
+CHAINS_A = 4
+COLS_A = CHAINS_A * WIDE
+PARTS = 2
+TIME_A, TIME_B = 4.6, 3.3
 
 NT = (((1,), (1,)), ((), ()))
 TN = (((0,), (0,)), ((), ()))
@@ -24,6 +27,16 @@
 
 def dot(a, b, dims=(((1,), (0,)), ((), ()))):
     return lax.dot_general(a, b, dims, preferred_element_type=F32)
+
+
+class Message:
+    def __init__(self, copy):
+        self.copy, self.got = copy, False
+
+    def wait_recv(self):
+        assert not self.got
+        self.got = True
+        self.copy.wait_recv()
 
 
 class Messages:
@@ -41,51 +54,48 @@
             device_id_type=MESH,
         )
         copy.start()
-        self.all.append(copy)
-        return copy
+        message = Message(copy)
+        self.all.append(message)
+        return message
 
 
 class Chain:
-    def __init__(self, net, pos, n, left, right, term, bufs):
-        self.net, self.pos, self.n, self.left, self.right, self.term = net, pos, n, left, right, term
-        self.send_r, self.recv_r, self.send_l, self.recv_l = bufs
-        self.hr, self.hl = n // 2, n - 1 - n // 2
-        self.mr, self.ml = [], []
+    def __init__(self, net, pos, n, sign, along, term, bufs):
+        self.net, self.pos, self.n, self.sign, self.term = net, pos, n, sign, term
+        self.far, self.near = n // 2, n - 1 - n // 2
+        send_f, recv_f, send_n, recv_n = bufs
+        self.ways = (
+            (sign, self.far, along(sign), send_f, recv_f, []),
+            (-sign, self.near, along(-sign), send_n, recv_n, []),
+        )
 
     def step(self, s):
-        if s < self.hr:
-            v = self.term(lax.rem(self.pos + self.hr - s, self.n))
+        for sign, hops, device, send, recv, sent in self.ways:
+            if s >= hops:
+                continue
+            v = self.term(lax.rem(self.pos + self.n + sign * (hops - s), self.n))
             if s:
-                self.mr[s - 1].wait_recv()
-                v = v + self.recv_r[s - 1].astype(F32)
-            self.send_r[s] = v.astype(BF16)
-            self.mr.append(self.net.start(self.send_r.at[s], self.recv_r.at[s], self.right))
-        if s < self.hl:
-            v = self.term(lax.rem(self.pos + self.n - self.hl + s, self.n))
-            if s:
-                self.ml[s - 1].wait_recv()
-                v = v + self.recv_l[s - 1].astype(F32)
-            self.send_l[s] = v.astype(BF16)
-            self.ml.append(self.net.start(self.send_l.at[s], self.recv_l.at[s], self.left))
+                sent[s - 1].wait_recv()
+                v = v + recv[s - 1].astype(F32)
+            send[s] = v.astype(BF16)
+            sent.append(self.net.start(send.at[s], recv.at[s], device))
 
     def final(self):
         v = self.term(self.pos)
-        self.mr[self.hr - 1].wait_recv()
-        v = v + self.recv_r[self.hr - 1].astype(F32)
-        if self.hl:
-            self.ml[self.hl - 1].wait_recv()
-            v = v + self.recv_l[self.hl - 1].astype(F32)
+        for sign, hops, device, send, recv, sent in self.ways:
+            sent[hops - 1].wait_recv()
+            v = v + recv[hops - 1].astype(F32)
         return v
 
 
 def kernel(
     nz, factor,
-    tok, cot, ids, wts, ew,
+    tok_h, cot_h, ids_h, wts_h, ew,
     lat_o, tg_o, rg_o, eg_o,
-    weights, tok_b, cot_b, route_b, pick_b, rhs_b, cot_s, grad_s,
+    tok, cot, ids, wts, weights, tok_b, cot_b, route_b, pick_b, rhs_b, cot_s, grad_s,
     con_l, con_g, sib_l, sib_g, part_l, part_g, xin, rg_s, rg_r,
     term_b, asr, arr, asl, arl, bsr, brr, bsl, brl, sum_a, sum_b, two_a, two_b, in_a, in_b,
-    local_sem, send_sems, recv_sems,
+    local_sems, send_sems, recv_sems,
 ):
     dp, ex = lax.axis_index("dp"), lax.axis_index("expert")
     z, y = lax.div(dp, NY), lax.rem(dp, NY)
@@ -103,15 +113,14 @@
     offset = (0, -1, 1, 2)
     inverse = (0, 2, 1, 3)
 
-    load = pltpu.make_async_copy(ew, weights, local_sem)
-    load.start()
-    expert_of = lax.broadcasted_iota(jnp.int32, (8, 128), 0)
-    w_in = wts[...].astype(F32)
-    id_in = ids[...]
-    route_b[0] = sum(
-        jnp.where(id_in[k : k + 1] == expert_of, w_in[k : k + 1], 0.0) for k in range(2)
-    )
-
+    loads = [
+        pltpu.make_async_copy(src, dst, local_sems.at[i])
+        for i, (src, dst) in enumerate(
+            ((ids_h, ids), (wts_h, wts), (tok_h, tok), (cot_h, cot), (ew, weights))
+        )
+    ]
+    for load in loads:
+        load.start()
     barrier = pltpu.get_barrier_semaphore()
     partners = (
         [in_group(offset[k % 4], k // 4) for k in range(1, 8)]
@@ -120,6 +129,16 @@
     )
     for device in partners:
         pl.semaphore_signal(barrier, inc=1, device_id=device, device_id_type=MESH)
+    for load in loads[:2]:
+        load.wait()
+    expert_of = lax.broadcasted_iota(jnp.int32, (8, 128), 0)
+    w_in = wts[...].astype(F32)
+    id_in = ids[...]
+    route_b[0] = sum(
+        jnp.where(id_in[k : k + 1] == expert_of, w_in[k : k + 1], 0.0) for k in range(2)
+    )
+    for load in loads[2:4]:
+        load.wait()
     pl.semaphore_wait(barrier, len(partners))
 
     net = Messages(send_sems, recv_sems)
@@ -137,6 +156,12 @@
     cot_l = net.start(cot, cot_b.at[0], right)
     tok_r = net.start(tok, tok_b.at[1], left)
 
+    def done():
+        for m in net.all:
+            if not m.got:
+                m.wait_recv()
+            m.copy.wait_send()
+
     def block(k):
         return (tok, cot) if k == 0 else (tok_b.at[k - 1], cot_b.at[k - 1])
 
@@ -148,7 +173,7 @@
     ).astype(F32)
     ranks = dot(jnp.where(rows > 0, 1.0, 0.0).astype(BF16), before.astype(BF16))
     seat = lax.broadcasted_iota(jnp.int32, (CAP, 128), 0).astype(F32)
-    load.wait()
+    loads[4].wait()
 
     def stage(slots, base):
         size = CAP * len(slots)
@@ -236,76 +261,112 @@
     stage((3, 7), 6 * CAP)
     to_sibling(3)
 
-    def term_of(i, carry):
-        at = pl.multiple_of(i * 128, 128)
-        t = dot(grad_s[:, pl.ds(at, 128)], rhs_b[lax.div(at, 2 * HID)], TN)
-        term_b[i] = t.reshape(NY, 16, t.shape[1])
-        return carry
-
-    lax.fori_loop(0, nz, term_of, 0)
-
-    wide_a, wide_b = asr.shape[-1], bsr.shape[-1]
+    def term_of(low, high):
+        def some_rows(i, carry):
+            at = pl.multiple_of(i * 128, 128)
+            t = dot(grad_s[:, pl.ds(at, 128)], rhs_b[lax.div(at, 2 * HID), :, low:high], TN)
+            term_b[i, :, :, low:high] = t.reshape(NY, 16, high - low)
+            return carry
+
+        lax.fori_loop(0, nz, some_rows, 0)
+
+    chains_b = term_b.shape[-1] // WIDE - CHAINS_A
 
     def chain_a(q):
         def term(t):
-            return term_b[:, t, :, q * wide_a : (q + 1) * wide_a]
+            return term_b[:, t, :, q * WIDE : (q + 1) * WIDE]
 
         bufs = [b.at[q] for b in (asr, arr, asl, arl)]
-        return Chain(net, y, NY, along_y(-1), along_y(1), term, bufs)
+        return Chain(net, y, NY, 1 - q % 2 * 2, along_y, term, bufs)
 
     def chain_b(q):
         def term(t):
-            return term_b[t, :, :, COLS_A + q * wide_b : COLS_A + (q + 1) * wide_b]
+            return term_b[t, :, :, COLS_A + q * WIDE : COLS_A + (q + 1) * WIDE]
 
         bufs = [b.at[q] for b in (bsr, brr, bsl, brl)]
-        return Chain(net, z, nz, along_z(-1), along_z(1), term, bufs)
-
-    chains_a = [chain_a(q) for q in range(SUBS)]
-    chains_b = [chain_b(q) for q in range(SUBS)]
-
-    def ring(s):
-        for q in range(SUBS):
-            chains_a[q].step(s)
-            chains_b[q].step(s)
-
-    ring(0)
-    chip_part(3)
-    far_l = net.start(part_l.at[3], xin.at[2], right)
-    far_g = net.start(part_g.at[3], xin.at[3], left)
-    rg_in = [
-        net.start(rg_s.at[k], rg_r.at[inverse[k % 4] + k // 4 * 4], in_group(offset[k % 4], k // 4))
-        for k in range(1, 8)
-    ]
-    ring(1)
-    ring(2)
-    far_l.wait_recv()
-    part_l[2] = (part_l[2].astype(F32) + xin[2].astype(F32)).astype(BF16)
-    last_l = net.start(part_l.at[2], xin.at[4], right)
-    far_g.wait_recv()
-    part_g[1] = (part_g[1].astype(F32) + xin[3].astype(F32)).astype(BF16)
-    last_g = net.start(part_g.at[1], xin.at[5], left)
-    ring(3)
-    chip_part(0)
-    for q in range(SUBS):
-        sum_a[:, :, q * wide_a : (q + 1) * wide_a] = chains_a[q].final()
-    two_a[...] = sum_a[...].astype(BF16)
-    a_in = [
-        net.start(two_a.at[lax.rem(z + d, nz)], in_a.at[d - 1], along_z(d)) for d in range(1, nz)
-    ]
-    for s in range(4, nz // 2):
-        ring(s)
-    for q in range(SUBS):
-        sum_b[:, :, q * wide_b : (q + 1) * wide_b] = chains_b[q].final()
-    two_b[...] = sum_b[...].astype(BF16)
-    b_in = [
-        net.start(two_b.at[lax.rem(y + d, NY)], in_b.at[d - 1], along_y(d)) for d in range(1, NY)
-    ]
+        return Chain(net, z, nz, 1 - q % 2 * 2, along_z, term, bufs)
+
+    def far_parts():
+        chip_part(3)
+        relay["far_l"] = net.start(part_l.at[3], xin.at[2], right)
+        relay["far_g"] = net.start(part_g.at[3], xin.at[3], left)
+        relay["route"] = [
+            net.start(rg_s.at[k], rg_r.at[inverse[k % 4] + k // 4 * 4], in_group(offset[k % 4], k // 4))
+            for k in range(1, 8)
+        ]
+
+    def last_parts():
+        relay["far_l"].wait_recv()
+        part_l[2] = (part_l[2].astype(F32) + xin[2].astype(F32)).astype(BF16)
+        relay["last_l"] = net.start(part_l.at[2], xin.at[4], right)
+        relay["far_g"].wait_recv()
+        part_g[1] = (part_g[1].astype(F32) + xin[3].astype(F32)).astype(BF16)
+        relay["last_g"] = net.start(part_g.at[1], xin.at[5], left)
+        chip_part(0)
+
+    def final_a(q):
+        v = all_a[q].final()
+        sum_a[:, :, q * WIDE : (q + 1) * WIDE] = v
+        two_a[:, :, q * WIDE : (q + 1) * WIDE] = v.astype(BF16)
+
+    def final_b(q):
+        v = all_b[q].final()
+        sum_b[:, :, q * WIDE : (q + 1) * WIDE] = v
+        two_b[:, :, q * WIDE : (q + 1) * WIDE] = v.astype(BF16)
+
+    def farthest_first(n):
+        return sorted(range(1, n), key=lambda d: -min(d, n - d))
+
+    def second_a(i):
+        cols = slice(i * COLS_A // PARTS, (i + 1) * COLS_A // PARTS)
+        a_in.extend(
+            net.start(two_a.at[lax.rem(z + d, nz), :, cols], in_a.at[d - 1, :, cols], along_z(d))
+            for d in farthest_first(nz)
+        )
+
+    def second_b(i):
+        wide = two_b.shape[-1]
+        cols = slice(i * wide // PARTS, (i + 1) * wide // PARTS)
+        b_in.extend(
+            net.start(two_b.at[lax.rem(y + d, NY), :, cols], in_b.at[d - 1, :, cols], along_y(d))
+            for d in farthest_first(NY)
+        )
+
+    a_in, b_in = [], []
+    relay = {}
+    all_a = [chain_a(q) for q in range(CHAINS_A)]
+    all_b = [chain_b(q) for q in range(chains_b)]
+    term_of(0, COLS_A)
+    for q in range(CHAINS_A):
+        all_a[q].step(0)
+    term_of(COLS_A, term_b.shape[-1])
+    for q in range(chains_b):
+        all_b[q].step(0)
+    events = [(0.0, far_parts), (2.5 * TIME_A, last_parts)]
+    for q in range(CHAINS_A):
+        for s in range(1, NY // 2):
+            events.append(((s + q / CHAINS_A) * TIME_A, lambda q=q, s=s: all_a[q].step(s)))
+        events.append(((NY // 2 + q / CHAINS_A) * TIME_A, lambda q=q: final_a(q)))
+    for q in range(chains_b):
+        for s in range(1, nz // 2):
+            events.append(((s + q / chains_b) * TIME_B, lambda q=q, s=s: all_b[q].step(s)))
+        events.append(((nz // 2 + q / chains_b) * TIME_B, lambda q=q: final_b(q)))
+    for i in range(PARTS):
+        last = (i + 1) * CHAINS_A // PARTS - 1
+        at = (NY // 2 + last / CHAINS_A) * TIME_A
+        events.append((at + 0.01, lambda i=i: second_a(i)))
+        last = (i + 1) * chains_b // PARTS - 1
+        at = (nz // 2 + last / chains_b) * TIME_B
+        events.append((at + 0.01, lambda i=i: second_b(i)))
+    for _, event in sorted(events, key=lambda e: e[0]):
+        event()
+    rg_in = relay["route"]
 
     near_g.wait_recv()
-    last_g.wait_recv()
+    relay["last_g"].wait_recv()
     tg_o[...] = (part_g[0].astype(F32) + xin[0].astype(F32) + xin[5].astype(F32)).astype(BF16)
     near_l.wait_recv()
-    last_l.wait_recv()
+    relay["last_l"].wait_recv()
     lat_o[...] = (part_l[0].astype(F32) + xin[1].astype(F32) + xin[4].astype(F32)).astype(BF16)
     route = [jnp.zeros((1, 128), F32), jnp.zeros((1, 128), F32)]
     for m in rg_in:
@@ -323,8 +384,12 @@
     for m in b_in:
         m.wait_recv()
     eg_o[:, COLS_A:] = factor * (sum_b[y] + jnp.sum(in_b[...].astype(F32), axis=0))
-    for m in net.all:
-        m.wait_send()
+    done()
+
+
+def pass_on(*refs):
+    for i in range(4):
+        refs[4 + i][...] = refs[i][...]
 
 
 def solution(mesh):
@@ -335,11 +400,11 @@
         count, width = tokens.shape
         slots = CAP * n_ex
         factor = 1.0 / math.sqrt(count * n_dp * n_ex)
-        wide_a, wide_b = COLS_A // SUBS, (width - COLS_A) // SUBS
+        chains_a, chains_b = CHAINS_A, width // WIDE - CHAINS_A
         hr_a, hl_a = NY // 2, NY - 1 - NY // 2
         hr_b, hl_b = nz // 2, nz - 1 - nz // 2
         vmem = pl.BlockSpec(memory_space=pltpu.VMEM)
-        count_messages = 7 + 6 + 6 + 2 + 8 + 6 + 7 + SUBS * (NY - 1 + nz - 1) + nz - 1 + NY - 1
+        count_messages = 7 + 6 + 6 + 2 + 8 + 6 + 7 + chains_a * (NY - 1) + chains_b * (nz - 1) + PARTS * (nz - 1 + NY - 1)
         lat, tg, rg, eg = pl.pallas_call(
             lambda *refs: kernel(nz, factor, *refs),
             out_shape=(
@@ -348,9 +413,13 @@
                 jax.ShapeDtypeStruct((2, count), F32),
                 jax.ShapeDtypeStruct((16, width), F32),
             ),
-            in_specs=[vmem, vmem, vmem, vmem, pl.BlockSpec(memory_space=pl.ANY)],
+            in_specs=[pl.BlockSpec(memory_space=pltpu.HBM)] * 5,
             out_specs=(vmem,) * 4,
             scratch_shapes=[
+                pltpu.VMEM((count, width), BF16),
+                pltpu.VMEM((count, width), BF16),
+                pltpu.VMEM((2, count), jnp.int32),
+                pltpu.VMEM((2, count), BF16),
                 pltpu.VMEM((3 * HID, width), BF16),
                 pltpu.VMEM((7, count, width), BF16),
                 pltpu.VMEM((7, count, width), BF16),
@@ -369,26 +438,26 @@
                 pltpu.VMEM((8, 8, 128), F32),
                 pltpu.VMEM((8, 8, 128), F32),
                 pltpu.VMEM((nz, NY, 16, width), F32),
-                pltpu.VMEM((SUBS, hr_a, nz, 16, wide_a), BF16),
-                pltpu.VMEM((SUBS, hr_a, nz, 16, wide_a), BF16),
-                pltpu.VMEM((SUBS, hl_a, nz, 16, wide_a), BF16),
-                pltpu.VMEM((SUBS, hl_a, nz, 16, wide_a), BF16),
-                pltpu.VMEM((SUBS, hr_b, NY, 16, wide_b), BF16),
-                pltpu.VMEM((SUBS, hr_b, NY, 16, wide_b), BF16),
-                pltpu.VMEM((SUBS, hl_b, NY, 16, wide_b), BF16),
-                pltpu.VMEM((SUBS, hl_b, NY, 16, wide_b), BF16),
+                pltpu.VMEM((chains_a, hr_a, nz, 16, WIDE), BF16),
+                pltpu.VMEM((chains_a, hr_a, nz, 16, WIDE), BF16),
+                pltpu.VMEM((chains_a, hl_a, nz, 16, WIDE), BF16),
+                pltpu.VMEM((chains_a, hl_a, nz, 16, WIDE), BF16),
+                pltpu.VMEM((chains_b, hr_b, NY, 16, WIDE), BF16),
+                pltpu.VMEM((chains_b, hr_b, NY, 16, WIDE), BF16),
+                pltpu.VMEM((chains_b, hl_b, NY, 16, WIDE), BF16),
+                pltpu.VMEM((chains_b, hl_b, NY, 16, WIDE), BF16),
                 pltpu.VMEM((nz, 16, COLS_A), F32),
                 pltpu.VMEM((NY, 16, width - COLS_A), F32),
                 pltpu.VMEM((nz, 16, COLS_A), BF16),
                 pltpu.VMEM((NY, 16, width - COLS_A), BF16),
                 pltpu.VMEM((nz - 1, 16, COLS_A), BF16),
                 pltpu.VMEM((NY - 1, 16, width - COLS_A), BF16),
-                pltpu.SemaphoreType.DMA,
+                pltpu.SemaphoreType.DMA((5,)),
                 pltpu.SemaphoreType.DMA((count_messages,)),
                 pltpu.SemaphoreType.DMA((count_messages,)),
             ],
             compiler_params=pltpu.CompilerParams(
-                collective_id=0, has_side_effects=True, vmem_limit_bytes=60 * 1024 * 1024
+                collective_id=0, has_side_effects=True, vmem_limit_bytes=62 * 1024 * 1024
             ),
         )(
             tokens,
@@ -397,6 +466,14 @@
             route_weights.T,
             expert_weights.reshape(expert_weights.shape[1:]),
         )
+        outs = (lat, tg, rg, eg)
+        lat, tg, rg, eg = pl.pallas_call(
+            pass_on,
+            out_shape=tuple(jax.ShapeDtypeStruct(o.shape, o.dtype) for o in outs),
+            in_specs=[vmem] * 4,
+            out_specs=(vmem,) * 4,
+            compiler_params=pltpu.CompilerParams(vmem_limit_bytes=62 * 1024 * 1024),
+        )(*outs)
         return lat, tg, rg.T, eg[None]
 
     return jax.shard_map(

time: 94.5 us -> 84.8 us (0.90)
  the two profiles are of different devices: /device:TPU:8 before, /device:TPU:64 now
where the time goes in v2:
time: 84.8 us; the launch traced here: 84.6 us
  Pallas kernels  84 us (99%)
    pallas_call x1, Pallas kernels, body(): pl.pallas_call(lambda *refs: kernel(nz, factor, *refs), out_shape=(jax.Sh...  82.1 us
    pallas_call x1, Pallas kernels, body(): pl.pallas_call(pass_on, out_shape=tuple((jax.ShapeDtypeStruct(o.shape, o....  1.86 us

profile of v2, /device:TPU:64, one launch (start us, length us, event | category | flops | bytes accessed | tf_op | source)
XLA Modules:
  0.0 84.6 jit_solution(2219635252591691179)
XLA Ops:
  0.6 82.1 %shard_map.84 = (bf16[128,1024]{1,0:T(8,128)(2,1)}, bf16[128,1024]{1,0:T(8,128)(2,1)}, f32[2,128]{1,0:T(2,128)}, f32[16,1024]{1,0:T(8,128)}) custom-call(bf16[128,1024]{1,0:T(8,128)(2,1)} %refs_0_.1, bf16[128,1024]{1,0:T(8,128)(2,1)} %refs_1_.1, s32[2,128]{1,0:T(2,128)} %bitcast.6, bf16[2,128]{1,0:T(2,128)(2,1)} %bitcast.7, bf16[1536,1024]{1,0:T(8,128)(2,1)} %bitcast.5), custom_call_target="tpu_custom_call" | custom-call | tf_op jit(solution)/shard_map/pallas_call | solution.py:408
  82.7 1.9 %shard_map.85 = (bf16[128,1024]{1,0:T(8,128)(2,1)}, bf16[128,1024]{1,0:T(8,128)(2,1)}, f32[2,128]{1,0:T(2,128)}, f32[16,1024]{1,0:T(8,128)}) custom-call(bf16[128,1024]{1,0:T(8,128)(2,1)} %get-tuple-element.12.refs_0_, bf16[128,1024]{1,0:T(8,128)(2,1)} %get-tuple-element.13.refs_1_, f32[2,128]{1,0:T(2,128)} %get-tuple-element.14.refs_2_, ...), custom_call_target="tpu_custom_call" | custom-call | tf_op jit(solution)/shard_map/pallas_call | solution.py:470

commit v3 on v2

v3 whole, which is shorter than its diff:
```python
import math

import jax
import jax.numpy as jnp
from jax import lax
from jax.experimental import pallas as pl
from jax.experimental.pallas import tpu as pltpu
from jax.sharding import PartitionSpec as P

MESH = pl.DeviceIdType.MESH
F32 = jnp.float32
BF16 = jnp.bfloat16

HID = 512
CAP = 64
NX = 4
NY = 8
ROWS = 512
WIDE = 128
PARTS_A = 2
PARTS_B = 2
CHAINS_A = 4
COLS_A = CHAINS_A * WIDE

NT = (((1,), (1,)), ((), ()))
TN = (((0,), (0,)), ((), ()))


def dot(a, b, dims=(((1,), (0,)), ((), ()))):
    return lax.dot_general(a, b, dims, preferred_element_type=F32)


class Messages:
    def __init__(self, send_sems, recv_sems):
        self.send_sems, self.recv_sems, self.index = send_sems, recv_sems, {}

    def make(self, key, src, dst, device):
        i = self.index.setdefault(key, len(self.index))
        return pltpu.make_async_remote_copy(
            src_ref=src,
            dst_ref=dst,
            send_sem=self.send_sems.at[i],
            recv_sem=self.recv_sems.at[i],
            device_id=device,
            device_id_type=MESH,
        )

    def start(self, key, src, dst, device):
        copy = self.make(key, src, dst, device)
        copy.start()
        return copy


class Chain:
    def __init__(self, net, key, pos, n, sign, along, term, bufs):
        self.net, self.pos, self.n, self.term = net, pos, n, term
        far, near = n // 2, n - 1 - n // 2
        send_f, recv_f, send_n, recv_n = bufs
        self.ways = (
            (key + ("far",), sign, far, along(sign), send_f, recv_f),
            (key + ("near",), -sign, near, along(-sign), send_n, recv_n),
        )

    def copy(self, way, s):
        key, _, _, device, send, recv = way
        return self.net.make(key + (s,), send.at[s], recv.at[s], device)

    def step(self, s):
        for way in self.ways:
            _, sign, hops, _, send, recv = way
            if s >= hops:
                continue
            values = self.term(lax.rem(self.pos + self.n + sign * (hops - s), self.n))
            if s:
                self.copy(way, s - 1).wait_recv()
            for e in range(2):
                v = values[e]
                if s:
                    v = v + recv[s - 1, e].astype(F32)
                send[s, e] = v.astype(BF16)
            self.copy(way, s).start()

    def final(self):
        values = self.term(self.pos)
        for way in self.ways:
            hops, recv = way[2], way[5]
            self.copy(way, hops - 1).wait_recv()
            values = [v + recv[hops - 1, e].astype(F32) for e, v in enumerate(values)]
        return values

    def sent(self):
        return [self.copy(way, s) for way in self.ways for s in range(way[2])]


def kernel(
    nz, factor,
    tok_h, cot_h, ids_h, wts_h, ew,
    lat_o, tg_o, rg_o, eg_o,
    tok, cot, ids, wts, weights, tok_b, cot_b, route_b, pick_b, rhs_b, cot_s, grad_s,
    con_l, con_g, sib_l, sib_g, part_l, part_g, xin, rg_s, rg_r,
    term_b, term_c, sib_b, eg_s, eg_r, asr, arr, asl, arl, bsr, brr, bsl, brl, sum_a, sum_b, two_a, two_b, in_a, in_b,
    local_sems, send_sems, recv_sems,
):
    dp, ex = lax.axis_index("dp"), lax.axis_index("expert")
    z, y = lax.div(dp, NY), lax.rem(dp, NY)
    x, c = lax.div(ex, 2), lax.rem(ex, 2)

    def in_group(dx, dc):
        return {"dp": dp, "expert": lax.rem(x + dx + NX, NX) * 2 + lax.rem(c + dc, 2)}

    def along_y(d):
        return {"dp": z * NY + lax.rem(y + d + NY, NY), "expert": ex}

    def along_z(d):
        return {"dp": lax.rem(z + d + nz, nz) * NY + y, "expert": ex}

    offset = (0, -1, 1, 2)
    inverse = (0, 2, 1, 3)

    loads = [
        pltpu.make_async_copy(src, dst, local_sems.at[i])
        for i, (src, dst) in enumerate(
            ((ids_h, ids), (wts_h, wts), (tok_h, tok), (cot_h, cot), (ew, weights))
        )
    ]
    for load in loads:
        load.start()
    barrier = pltpu.get_barrier_semaphore()
    def farthest_first(n):
        return sorted(range(1, n), key=lambda d: -min(d, n - d))

    group = [in_group(offset[k % 4], k // 4) for k in range(1, 8)]
    partners_0 = [along_z(d) for d in farthest_first(nz)] + [along_y(1), along_y(-1)] + group
    partners_1 = [along_y(d) for d in farthest_first(NY)] + [along_z(1), along_z(-1)] + group

    def greet(partners):
        for device in partners:
            pl.semaphore_signal(barrier, inc=1, device_id=device, device_id_type=MESH)

    pl.when(c == 0)(lambda: greet(partners_0))
    pl.when(c == 1)(lambda: greet(partners_1))
    for load in loads[:2]:
        load.wait()
    expert_of = lax.broadcasted_iota(jnp.int32, (8, 128), 0)
    w_in = wts[...].astype(F32)
    id_in = ids[...]
    route_b[0] = sum(
        jnp.where(id_in[k : k + 1] == expert_of, w_in[k : k + 1], 0.0) for k in range(2)
    )
    for load in loads[2:4]:
        load.wait()
    pl.semaphore_wait(barrier, jnp.where(c == 0, len(partners_0), len(partners_1)))

    net = Messages(send_sems, recv_sems)
    right, left, sibling = in_group(1, 0), in_group(-1, 0), in_group(0, 1)

    route_in = [
        net.start(("route", k), route_b.at[0], route_b.at[inverse[k % 4] + k // 4 * 4], in_group(offset[k % 4], k // 4))
        for k in range(1, 8)
    ]
    sib_t, sib_c = [None] * 4, [None] * 4
    tok_l = net.start(("c", 1), tok, tok_b.at[0], right)
    cot_r = net.start(("c", 2), cot, cot_b.at[1], left)
    sib_t[0] = net.start(("c", 3), tok, tok_b.at[3], sibling)
    sib_c[0] = net.start(("c", 4), cot, cot_b.at[3], sibling)

    def block(k):
        return (tok, cot) if k == 0 else (tok_b.at[k - 1], cot_b.at[k - 1])

    for m in route_in:
        m.wait_recv()
    rows = jnp.concatenate([route_b[k, pl.ds(ex, 1), :] for k in range(8)], axis=0)
    before = (
        lax.broadcasted_iota(jnp.int32, (128, 128), 0) < lax.broadcasted_iota(jnp.int32, (128, 128), 1)
    ).astype(F32)
    ranks = dot(jnp.where(rows > 0, 1.0, 0.0).astype(BF16), before.astype(BF16))
    seat = lax.broadcasted_iota(jnp.int32, (CAP, 128), 0).astype(F32)
    loads[4].wait()

    def stage(slots, base):
        size = CAP * len(slots)
        own = pl.ds(base, size)
        w_of = []
        for i, k in enumerate(slots):
            at = pl.ds(base + CAP * i, CAP)
            pick = jnp.where((ranks[k : k + 1] == seat) & (rows[k : k + 1] > 0), 1.0, 0.0)
            w = jnp.sum(pick * rows[k : k + 1], axis=1, keepdims=True)
            w_of.append(w)
            pick = pick.astype(BF16)
            pick_b[k] = pick
            t_ref, c_ref = block(k)
            rhs_b[0, at, :] = dot(pick, t_ref[...]).astype(BF16)
            cots = dot(pick, c_ref[...])
            cot_s[at, :] = cots.astype(BF16)
            rhs_b[1, at, :] = (w * cots).astype(BF16)
        w = jnp.concatenate(w_of, axis=0)
        both = dot(rhs_b[0, own, :], weights[: 2 * HID, :], NT)
        gate, up = both[:, :HID], both[:, HID:]
        sig = 1.0 / (1.0 + jnp.exp(-gate))
        act = gate * sig
        hidden = (act * up).astype(BF16)
        grad_s[own, 2 * HID :] = hidden
        d_hidden = dot(rhs_b[1, own, :], weights[2 * HID :, :], NT)
        grad_s[own, HID : 2 * HID] = (d_hidden * act).astype(BF16)
        grad_s[own, :HID] = (d_hidden * up * sig * (1.0 + gate * (1.0 - sig))).astype(BF16)
        out = dot(hidden, weights[2 * HID :, :]).astype(BF16).astype(F32)
        r_grad = jnp.sum(cot_s[own, :].astype(F32) * out, axis=1, keepdims=True)
        out = (w * out).astype(BF16)
        d_x = dot(grad_s[own, : 2 * HID], weights[: 2 * HID, :]).astype(BF16)
        for i, k in enumerate(slots):
            pick = pick_b[k]
            part = slice(CAP * i, CAP * (i + 1))
            con_l[k] = dot(pick, out[part], TN).astype(BF16)
            con_g[k] = dot(pick, d_x[part], TN).astype(BF16)
            line = jnp.sum(pick.astype(F32) * r_grad[part], axis=0, keepdims=True)
            rg_s[k] = jnp.broadcast_to(line, (8, 128))

    sib_out = {}

    def to_sibling(k):
        sib_out[k] = (
            net.start(("sib_l", k), con_l.at[k + 4], sib_l.at[k], sibling),
            net.start(("sib_g", k), con_g.at[k + 4], sib_g.at[k], sibling),
        )

    def chip_part(k):
        for m in sib_out[k]:
            m.wait_recv()
        part_l[k] = (con_l[k].astype(F32) + sib_l[k].astype(F32)).astype(BF16)
        part_g[k] = (con_g[k].astype(F32) + sib_g[k].astype(F32)).astype(BF16)

    sib_t[0].wait_recv()
    sib_c[0].wait_recv()
    stage((0, 4), 0)
    cot_l = net.start(("c", 5), cot, cot_b.at[0], right)
    tok_r = net.start(("c", 6), tok, tok_b.at[1], left)
    to_sibling(0)

    tok_l.wait_recv()
    opp_t = net.start(("c", 7), tok_b.at[0], tok_b.at[2], right)
    sib_t[1] = net.start(("c", 8), tok_b.at[0], tok_b.at[4], sibling)
    cot_r.wait_recv()
    opp_c = net.start(("c", 9), cot_b.at[1], cot_b.at[2], left)
    sib_c[2] = net.start(("c", 10), cot_b.at[1], cot_b.at[5], sibling)
    cot_l.wait_recv()
    sib_c[1] = net.start(("c", 11), cot_b.at[0], cot_b.at[4], sibling)
    tok_r.wait_recv()
    sib_t[2] = net.start(("c", 12), tok_b.at[1], tok_b.at[5], sibling)
    for k in (1, 2):
        sib_t[k].wait_recv()
        sib_c[k].wait_recv()
    stage((1, 2, 5, 6), 2 * CAP)
    to_sibling(1)
    to_sibling(2)
    opp_t.wait_recv()
    sib_t[3] = net.start(("c", 13), tok_b.at[2], tok_b.at[6], sibling)
    opp_c.wait_recv()
    sib_c[3] = net.start(("c", 14), cot_b.at[2], cot_b.at[6], sibling)
    chip_part(1)
    chip_part(2)
    near_g = net.start(("c", 15), part_g.at[2], xin.at[0], right)
    near_l = net.start(("c", 16), part_l.at[1], xin.at[1], left)

    sib_t[3].wait_recv()
    sib_c[3].wait_recv()
    stage((3, 7), 6 * CAP)
    to_sibling(3)

    early = [*route_in, tok_l, cot_l, tok_r, cot_r, *sib_t, *sib_c, opp_t, opp_c, near_g, near_l]
    early += [m for pair in sib_out.values() for m in pair]

    half = nz // 2
    wide = term_b.shape[-1]
    chains_b = wide // WIDE - CHAINS_A

    def rows_of(low, high):
        def some_rows(i, carry):
            at = pl.multiple_of(i * ROWS, ROWS)
            v = dot(grad_s[:, pl.ds(at, ROWS)], rhs_b[lax.div(at, 2 * HID), :, low:high], TN)
            v = v.reshape(ROWS // 128, NY, 16, high - low)
            own = pl.ds(i * (ROWS // 128), ROWS // 128)
            term_b[own, :, :, low:high] = v
            term_c[own, :, :, low:high] = v.astype(BF16)
            return carry

        lax.fori_loop(0, 3 * HID // ROWS, some_rows, 0)

    def order(i):
        d = 0 if i == nz - 1 else half - (i + 1) // 2 if i % 2 else half + i // 2
        return lax.rem(z + d, nz)

    def term_of_b(i):
        t = order(i)
        part = (t, slice(None), slice(None), slice(COLS_A, wide))
        return net.make(("term_b", i), term_c.at[part], sib_b.at[part], sibling)

    def term_of_a(q):
        part = (slice(None), slice(None), slice(None), slice(q * WIDE, (q + 1) * WIDE))
        return net.make(("term_a", q), term_c.at[part], sib_b.at[part], sibling)

    def chain_a(q):
        cols = slice(q * WIDE, (q + 1) * WIDE)

        def term(t):
            return [term_b[:, t, :, cols], sib_b[:, t, :, cols].astype(F32)]

        bufs = [b.at[q] for b in (asr, arr, asl, arl)]
        return Chain(net, ("A", q), y, NY, 1 - q % 2 * 2, along_y, term, bufs)

    def chain_b(q):
        cols = slice(COLS_A + q * WIDE, COLS_A + (q + 1) * WIDE)

        def term(t):
            return [sib_b[t, :, :, cols].astype(F32), term_b[t, :, :, cols]]

        bufs = [b.at[q] for b in (bsr, brr, bsl, brl)]
        return Chain(net, ("B", q), z, nz, 1 - q % 2 * 2, along_z, term, bufs)

    all_a = [chain_a(q) for q in range(CHAINS_A)]
    all_b = [chain_b(q) for q in range(chains_b)]

    rows_of(0, wide)

    def send_a():
        for q in range(CHAINS_A):
            term_of_a(q).start()

    pl.when(c == 1)(send_a)
    def send_b():
        for i in range(nz):
            term_of_b(i).start()

    pl.when(c == 0)(send_b)

    def far_l():
        return net.make("far_l", part_l.at[3], xin.at[2], right)

    def far_g():
        return net.make("far_g", part_g.at[3], xin.at[3], left)

    def last_l():
        return net.make("last_l", part_l.at[2], xin.at[4], right)

    def last_g():
        return net.make("last_g", part_g.at[1], xin.at[5], left)

    def route_out(k):
        to = inverse[k % 4] + k // 4 * 4
        return net.make(("rg", k), rg_s.at[k], rg_r.at[to], in_group(offset[k % 4], k // 4))

    def far_parts():
        chip_part(3)
        far_l().start()
        far_g().start()
        for k in range(1, 8):
            route_out(k).start()

    def last_parts():
        far_l().wait_recv()
        part_l[2] = (part_l[2].astype(F32) + xin[2].astype(F32)).astype(BF16)
        last_l().start()
        far_g().wait_recv()
        part_g[1] = (part_g[1].astype(F32) + xin[3].astype(F32)).astype(BF16)
        last_g().start()
        chip_part(0)

    def outputs():
        near_g.wait_recv()
        last_g().wait_recv()
        tg_o[...] = (part_g[0].astype(F32) + xin[0].astype(F32) + xin[5].astype(F32)).astype(BF16)
        near_l.wait_recv()
        last_l().wait_recv()
        lat_o[...] = (part_l[0].astype(F32) + xin[1].astype(F32) + xin[4].astype(F32)).astype(BF16)
        route = [jnp.zeros((1, 128), F32), jnp.zeros((1, 128), F32)]
        for k in range(1, 8):
            route_out(k).wait_recv()
        for k in range(8):
            line = rg_s[0, 0:1, :] if k == 0 else rg_r[k, 0:1, :]
            expert = in_group(offset[k % 4], k // 4)["expert"]
            for j in range(2):
                route[j] = route[j] + jnp.where(id_in[j : j + 1] == expert, line, 0.0)
        rg_o[...] = jnp.concatenate(route, axis=0)
        for m in (far_l(), far_g(), last_l(), last_g(), *(route_out(k) for k in range(1, 8))):
            m.wait_send()

    def share(low, high):
        part = (slice(None), slice(low, high))
        return net.make(("share", low), eg_s.at[part], eg_r.at[part], sibling)

    def run(events):
        for _, event in sorted(events, key=lambda e: e[0]):
            event()

    def finish(own, summed, place, incoming, arrived, low, high):
        outputs()
        for m in incoming:
            m.wait_recv()
        for e in (1 - own, own):
            total = factor * (summed[place, e] + jnp.sum(arrived[:, e].astype(F32), axis=0))
            if e == own:
                eg_o[:, low:high] = total
            else:
                eg_s[:, low:high] = total
                to_other = share(low, high)
                to_other.start()
        other = (COLS_A, wide) if low == 0 else (0, COLS_A)
        for m in incoming:
            m.wait_send()
        share(*other).wait_recv()
        eg_o[:, other[0] : other[1]] = eg_r[:, other[0] : other[1]]
        to_other.wait_send()

    def core_0():
        a_in = []

        def first(q):
            term_of_a(q).wait_recv()
            all_a[q].step(0)

        def final(q):
            cols = slice(q * WIDE, (q + 1) * WIDE)
            for e, v in enumerate(all_a[q].final()):
                sum_a[:, e, :, cols] = v
                two_a[:, e, :, cols] = v.astype(BF16)

        def second(i):
            cols = slice(i * COLS_A // PARTS_A, (i + 1) * COLS_A // PARTS_A)
            a_in.extend(
                net.start(("a", i, d), two_a.at[lax.rem(z + d, nz), :, :, cols], in_a.at[d - 1, :, :, cols], along_z(d))
                for d in farthest_first(nz)
            )

        events = [(0.99, far_parts), (2.3, last_parts)]
        for q in range(CHAINS_A):
            events.append((q / CHAINS_A, lambda q=q: first(q)))
            for s in range(1, NY // 2):
                events.append((s + q / CHAINS_A, lambda q=q, s=s: all_a[q].step(s)))
            events.append((NY // 2 + q / CHAINS_A, lambda q=q: final(q)))
        for i in range(PARTS_A):
            last = (i + 1) * CHAINS_A // PARTS_A - 1
            events.append((NY // 2 + last / CHAINS_A + 0.01, lambda i=i: second(i)))
        run(events)
        finish(0, sum_a, z, a_in, in_a, 0, COLS_A)
        for m in [term_of_b(i) for i in range(nz)] + [m for chain in all_a for m in chain.sent()]:
            m.wait_send()

    def core_1():
        b_in = []

        def step(q, s):
            if q == 0:
                for i in (2 * s + 1, 2 * s + 2) if s else (0, 1, 2):
                    if i < nz:
                        term_of_b(i).wait_recv()
            all_b[q].step(s)

        def final(q):
            cols = slice(q * WIDE, (q + 1) * WIDE)
            for e, v in enumerate(all_b[q].final()):
                sum_b[:, e, :, cols] = v
                two_b[:, e, :, cols] = v.astype(BF16)

        def second(i):
            cols = slice(i * (wide - COLS_A) // PARTS_B, (i + 1) * (wide - COLS_A) // PARTS_B)
            b_in.extend(
                net.start(("b", i, d), two_b.at[lax.rem(y + d, NY), :, :, cols], in_b.at[d - 1, :, :, cols], along_y(d))
                for d in farthest_first(NY)
            )

        events = [(0.99, far_parts), (3.3, last_parts)]
        for q in range(chains_b):
            for s in range(half):
                events.append((s + q / chains_b, lambda q=q, s=s: step(q, s)))
            events.append((half + q / chains_b, lambda q=q: final(q)))
        for i in range(PARTS_B):
            last = (i + 1) * chains_b // PARTS_B - 1
            events.append((half + last / chains_b + 0.01, lambda i=i: second(i)))
        run(events)
        finish(1, sum_b, y, b_in, in_b, COLS_A, wide)
        for m in [term_of_a(q) for q in range(CHAINS_A)] + [m for chain in all_b for m in chain.sent()]:
            m.wait_send()

    pl.when(c == 0)(core_0)
    pl.when(c == 1)(core_1)
    for m in early:
        m.wait_send()


def pass_on(*refs):
    for i in range(4):
        refs[4 + i][...] = refs[i][...]


def solution(mesh):
    n_dp, n_ex = mesh.shape["dp"], mesh.shape["expert"]
    nz = n_dp // NY

    def body(tokens, cotangent, expert_ids, route_weights, expert_weights):
        count, width = tokens.shape
        slots = CAP * n_ex
        factor = 1.0 / math.sqrt(count * n_dp * n_ex)
        chains_a, chains_b = CHAINS_A, width // WIDE - CHAINS_A
        hr_a, hl_a = NY // 2, NY - 1 - NY // 2
        hr_b, hl_b = nz // 2, nz - 1 - nz // 2
        vmem = pl.BlockSpec(memory_space=pltpu.VMEM)
        count_messages = 7 + 6 + 6 + 2 + 8 + 6 + 7 + 2 + nz + chains_a + chains_a * (NY - 1) + chains_b * (nz - 1) + PARTS_A * (nz - 1) + PARTS_B * (NY - 1)
        lat, tg, rg, eg = pl.pallas_call(
            lambda *refs: kernel(nz, factor, *refs),
            out_shape=(
                jax.ShapeDtypeStruct((count, width), BF16),
                jax.ShapeDtypeStruct((count, width), BF16),
                jax.ShapeDtypeStruct((2, count), F32),
                jax.ShapeDtypeStruct((16, width), F32),
            ),
            in_specs=[pl.BlockSpec(memory_space=pltpu.HBM)] * 5,
            out_specs=(vmem,) * 4,
            scratch_shapes=[
                pltpu.VMEM((count, width), BF16),
                pltpu.VMEM((count, width), BF16),
                pltpu.VMEM((2, count), jnp.int32),
                pltpu.VMEM((2, count), BF16),
                pltpu.VMEM((3 * HID, width), BF16),
                pltpu.VMEM((7, count, width), BF16),
                pltpu.VMEM((7, count, width), BF16),
                pltpu.VMEM((8, 8, 128), F32),
                pltpu.VMEM((8, CAP, 128), BF16),
                pltpu.VMEM((2, slots, width), BF16),
                pltpu.VMEM((slots, width), BF16),
                pltpu.VMEM((slots, 3 * HID), BF16),
                pltpu.VMEM((8, count, width), BF16),
                pltpu.VMEM((8, count, width), BF16),
                pltpu.VMEM((4, count, width), BF16),
                pltpu.VMEM((4, count, width), BF16),
                pltpu.VMEM((4, count, width), BF16),
                pltpu.VMEM((4, count, width), BF16),
                pltpu.VMEM((6, count, width), BF16),
                pltpu.VMEM((8, 8, 128), F32),
                pltpu.VMEM((8, 8, 128), F32),
                pltpu.VMEM((nz, NY, 16, width), F32),
                pltpu.VMEM((nz, NY, 16, width), BF16),
                pltpu.VMEM((nz, NY, 16, width), BF16),
                pltpu.VMEM((16, width), F32),
                pltpu.VMEM((16, width), F32),
                pltpu.VMEM((chains_a, hr_a, 2, nz, 16, WIDE), BF16),
                pltpu.VMEM((chains_a, hr_a, 2, nz, 16, WIDE), BF16),
                pltpu.VMEM((chains_a, hl_a, 2, nz, 16, WIDE), BF16),
                pltpu.VMEM((chains_a, hl_a, 2, nz, 16, WIDE), BF16),
                pltpu.VMEM((chains_b, hr_b, 2, NY, 16, WIDE), BF16),
                pltpu.VMEM((chains_b, hr_b, 2, NY, 16, WIDE), BF16),
                pltpu.VMEM((chains_b, hl_b, 2, NY, 16, WIDE), BF16),
                pltpu.VMEM((chains_b, hl_b, 2, NY, 16, WIDE), BF16),
                pltpu.VMEM((nz, 2, 16, COLS_A), F32),
                pltpu.VMEM((NY, 2, 16, width - COLS_A), F32),
                pltpu.VMEM((nz, 2, 16, COLS_A), BF16),
                pltpu.VMEM((NY, 2, 16, width - COLS_A), BF16),
                pltpu.VMEM((nz - 1, 2, 16, COLS_A), BF16),
                pltpu.VMEM((NY - 1, 2, 16, width - COLS_A), BF16),
                pltpu.SemaphoreType.DMA((5,)),
                pltpu.SemaphoreType.DMA((count_messages,)),
                pltpu.SemaphoreType.DMA((count_messages,)),
            ],
            compiler_params=pltpu.CompilerParams(
                collective_id=0, has_side_effects=True, vmem_limit_bytes=62 * 1024 * 1024
            ),
        )(
            tokens,
            cotangent,
            expert_ids.T,
            route_weights.T,
            expert_weights.reshape(expert_weights.shape[1:]),
        )
        outs = (lat, tg, rg, eg)
        lat, tg, rg, eg = pl.pallas_call(
            pass_on,
            out_shape=tuple(jax.ShapeDtypeStruct(o.shape, o.dtype) for o in outs),
            in_specs=[vmem] * 4,
            out_specs=(vmem,) * 4,
            compiler_params=pltpu.CompilerParams(vmem_limit_bytes=62 * 1024 * 1024),
        )(*outs)
        return lat, tg, rg.T, eg[None]

    return jax.shard_map(
        body,
        mesh=mesh,
        in_specs=(
            P(("dp", "expert"), None),
            P(("dp", "expert"), None),
            P(("dp", "expert"), None),
            P(("dp", "expert"), None),
            P("expert", None, None),
        ),
        out_specs=(
            P(("dp", "expert"), None),
            P(("dp", "expert"), None),
            P(("dp", "expert"), None),
            P("expert", "dp", None),
        ),
        check_vma=False,
    )
```

time: 84.8 us -> 83.7 us (0.987)
  the two profiles are of different devices: /device:TPU:64 before, /device:TPU:1 now
where the time goes in v3:
time: 83.7 us; the launch traced here: 83.5 us
  Pallas kernels  82.9 us (99%)
    pallas_call x1, Pallas kernels, body(): pl.pallas_call(lambda *refs: kernel(nz, factor, *refs), out_shape=(jax.Sh...  81 us
    pallas_call x1, Pallas kernels, body(): pl.pallas_call(pass_on, out_shape=tuple((jax.ShapeDtypeStruct(o.shape, o....  1.86 us

profile of v3, /device:TPU:1, one launch (start us, length us, event | category | flops | bytes accessed | tf_op | source)
XLA Modules:
  0.0 83.5 jit_solution(5071052171766297261)
XLA Ops:
  0.6 81.0 %shard_map.84 = (bf16[128,1024]{1,0:T(8,128)(2,1)}, bf16[128,1024]{1,0:T(8,128)(2,1)}, f32[2,128]{1,0:T(2,128)}, f32[16,1024]{1,0:T(8,128)}) custom-call(bf16[128,1024]{1,0:T(8,128)(2,1)} %refs_0_.1, bf16[128,1024]{1,0:T(8,128)(2,1)} %refs_1_.1, s32[2,128]{1,0:T(2,128)} %bitcast.6, bf16[2,128]{1,0:T(2,128)(2,1)} %bitcast.7, bf16[1536,1024]{1,0:T(8,128)(2,1)} %bitcast.5), custom_call_target="tpu_custom_call" | custom-call | tf_op jit(solution)/shard_map/pallas_call | solution.py:507
  81.7 1.9 %shard_map.85 = (bf16[128,1024]{1,0:T(8,128)(2,1)}, bf16[128,1024]{1,0:T(8,128)(2,1)}, f32[2,128]{1,0:T(2,128)}, f32[16,1024]{1,0:T(8,128)}) custom-call(bf16[128,1024]{1,0:T(8,128)(2,1)} %get-tuple-element.12.refs_0_, bf16[128,1024]{1,0:T(8,128)(2,1)} %get-tuple-element.13.refs_1_, f32[2,128]{1,0:T(2,128)} %get-tuple-element.14.refs_2_, ...), custom_call_target="tpu_custom_call" | custom-call | tf_op jit(solution)/shard_map/pallas_call | solution.py:573

commit v4 on v3

--- a/solution.py
+++ b/solution.py
@@ -154,15 +154,15 @@
     net = Messages(send_sems, recv_sems)
     right, left, sibling = in_group(1, 0), in_group(-1, 0), in_group(0, 1)
 
-    route_in = [
-        net.start(("route", k), route_b.at[0], route_b.at[inverse[k % 4] + k // 4 * 4], in_group(offset[k % 4], k // 4))
-        for k in range(1, 8)
-    ]
     sib_t, sib_c = [None] * 4, [None] * 4
     tok_l = net.start(("c", 1), tok, tok_b.at[0], right)
     cot_r = net.start(("c", 2), cot, cot_b.at[1], left)
     sib_t[0] = net.start(("c", 3), tok, tok_b.at[3], sibling)
     sib_c[0] = net.start(("c", 4), cot, cot_b.at[3], sibling)
+    route_in = [
+        net.start(("route", k), route_b.at[0], route_b.at[inverse[k % 4] + k // 4 * 4], in_group(offset[k % 4], k // 4))
+        for k in range(1, 8)
+    ]
 
     def block(k):
         return (tok, cot) if k == 0 else (tok_b.at[k - 1], cot_b.at[k - 1])

time: 83.7 us -> 88.7 us (1.060)
  Pallas kernels: 82.9 us -> 88 us
    pallas_call x1, Pallas kernels: 81 us -> 86.1 us  [body(): pl.pallas_call(lambda *refs: kernel(nz, factor, *refs), out_shape=(jax.Sh...]
where the time goes in v4:
time: 88.7 us; the launch traced here: 88.6 us
  Pallas kernels  88 us (99%)
    pallas_call x1, Pallas kernels, body(): pl.pallas_call(lambda *refs: kernel(nz, factor, *refs), out_shape=(jax.Sh...  86.1 us
    pallas_call x1, Pallas kernels, body(): pl.pallas_call(pass_on, out_shape=tuple((jax.ShapeDtypeStruct(o.shape, o....  1.86 us

profile of v4, /device:TPU:1, one launch (start us, length us, event | category | flops | bytes accessed | tf_op | source)
XLA Modules:
  0.0 88.6 jit_solution(17277101948878890241)
XLA Ops:
  0.6 86.1 %shard_map.84 = (bf16[128,1024]{1,0:T(8,128)(2,1)}, bf16[128,1024]{1,0:T(8,128)(2,1)}, f32[2,128]{1,0:T(2,128)}, f32[16,1024]{1,0:T(8,128)}) custom-call(bf16[128,1024]{1,0:T(8,128)(2,1)} %refs_0_.1, bf16[128,1024]{1,0:T(8,128)(2,1)} %refs_1_.1, s32[2,128]{1,0:T(2,128)} %bitcast.6, bf16[2,128]{1,0:T(2,128)(2,1)} %bitcast.7, bf16[1536,1024]{1,0:T(8,128)(2,1)} %bitcast.5), custom_call_target="tpu_custom_call" | custom-call | tf_op jit(solution)/shard_map/pallas_call | solution.py:507
  86.7 1.9 %shard_map.85 = (bf16[128,1024]{1,0:T(8,128)(2,1)}, bf16[128,1024]{1,0:T(8,128)(2,1)}, f32[2,128]{1,0:T(2,128)}, f32[16,1024]{1,0:T(8,128)}) custom-call(bf16[128,1024]{1,0:T(8,128)(2,1)} %get-tuple-element.12.refs_0_, bf16[128,1024]{1,0:T(8,128)(2,1)} %get-tuple-element.13.refs_1_, f32[2,128]{1,0:T(2,128)} %get-tuple-element.14.refs_2_, ...), custom_call_target="tpu_custom_call" | custom-call | tf_op jit(solution)/shard_map/pallas_call | solution.py:573
